TPU v7x, 128 devices: a whole 4x4x4 slice. The times are simulated.
128 devices in a mesh: row: 16 (over y, x), col: 8 (over z, core).
Axes of the slice: x: 4, y: 4, z: 4, core: 2. Of those that a mesh axis runs over, the one named last changes fastest.
Arguments:
- amplitudes: bfloat16 [4096, 8, 1024], P('col', None, 'row'), may hold values from -6 to 6
- integrals: bfloat16 [8, 1024, 16384], P(None, 'col', 'row'), may hold values from -0.1875 to 0.1875
- cd_count: int32 [8], replicated, may hold values from 1 to 1024, 6144 in all
- ab_count: int32 [8], replicated, may hold values from 1 to 8192, 49152 in all
Outputs:
- ladder: bfloat16 [4096, 8, 16384], P('col', None, 'row')
Inputs may be any that keep to these rules, and one draw needn't show every extreme that they name: `cd_count`: the counts sum to 6144, and the largest is 1024. `ab_count`: the counts sum to 49152, and the largest is 8192.
All inputs are finite; a program needn't handle non-finite values.
Results may differ from a plain program's by a relative error of at most 0.001.
Values may be sent and summed in bfloat16 or wider, within the bound.
A program may use at most 192 MiB of HBM per device.

v0:
```python
import jax
import jax.numpy as jnp
from jax import lax
from jax.sharding import PartitionSpec as P


def partner(array, axis, bit):
    return lax.ppermute(array, axis, [(i, i ^ 1 << bit) for i in range(lax.axis_size(axis))])


def per_device(amplitudes, integrals, cd_count, ab_count):
    row_count = lax.axis_size("row")
    swap_bit = row_count.bit_length() - 2
    local_width = integrals.shape[2]
    half_slots = local_width * row_count // 2
    amp_full = lax.all_gather(amplitudes, "row", axis=2, tiled=True)
    slots = lax.broadcasted_iota(jnp.int32, amp_full.shape[1:], 1)
    live = slots < cd_count[:, None]
    live_amps = jnp.where(live[None], amp_full, jnp.zeros_like(amp_full))
    places = lax.axis_index("row") * local_width + lax.broadcasted_iota(
        jnp.int32, (amp_full.shape[1], local_width), 1
    )
    keep = places % half_slots < ab_count[:, None]
    direct = jnp.einsum(
        "oik,ikn->oin",
        live_amps,
        lax.all_gather(integrals, "col", axis=1, tiled=True),
        preferred_element_type=jnp.float32,
    )
    mirrored = partner(direct, "row", swap_bit)
    difference = direct - mirrored
    return jnp.where(keep[None], difference, jnp.zeros_like(difference)).astype(jnp.bfloat16)


def solution(mesh):
    in_specs = (P("col", None, "row"), P(None, "col", "row"), P(), P())
    out_specs = P("col", None, "row")
    return jax.shard_map(
        per_device, mesh=mesh, in_specs=in_specs, out_specs=out_specs, check_vma=False
    )
```

profile of v0, /device:TPU:1, one launch (start us, length us, event | category | flops | bytes accessed | tf_op | source)
XLA Modules:
  0.0 584.6 jit_solution(13096501879292128270)
XLA Ops:
  6.5 0.0 all-gather.3.cloned.1.call-start
  6.5 0.7 all-gather.3.cloned.1.call-update
  7.3 0.0 all-gather.5.cloned.1.call-start
  7.3 0.7 all-gather.5.cloned.1.call-update
  8.0 0.7 iota_compare_fusion
  8.7 0.0 copy-start
  8.7 74.6 %all-gather.3.cloned.1.call-done = bf16[512,8,1024]{0,2,1:T(8,128)(2,1)} async-done(((bf16[512,8,64]{0,2,1:T(8,128)(2,1)}), bf16[512,8,1024]{0,2,1:T(8,128)(2,1)}) %all-gather.3.cloned.1.call-update) | async-done | bytes 8388624 | tf_op jit(solution)/shard_map/all_gather | solution.py:16
  83.4 87.0 %all-gather.5.cloned.1.call-done = bf16[8,1024,1024]{2,1,0:T(8,128)(2,1)} async-done(((bf16[8,128,1024]{2,1,0:T(8,128)(2,1)}), bf16[8,1024,1024]{2,1,0:T(8,128)(2,1)}) %all-gather.5.cloned.1.call-update) | async-done | bytes 16777232 | tf_op jit(solution)/shard_map/all_gather | solution.py:27
  170.4 17.4 %convolution_bitcast_fusion = f32[512,8,1024]{2,0,1:T(8,128)} fusion(bf16[8,1024,1024]{2,1,0:T(8,128)(2,1)} %all-gather.5.cloned.1.call-done, bf16[512,8,1024]{0,2,1:T(8,128)(2,1)} %all-gather.3.cloned.1.call-done, pred[8,1024]{1,0:T(8,128)(4,1)S(1)} %iota_compare_fusion), kind=kOutput, calls=%fused_computation.1 | convolution fusion | flops 8594128896 | bytes 41951232 | tf_op jit(solution)/shard_map/oik,ikn->oin/dot_general | solution.py:24
  187.7 2.7 collective-permute-start
  190.5 0.0 copy-done
  190.5 0.1 select_compare_fusion
  190.6 360.5 %collective-permute-done = f32[512,8,1024]{2,0,1:T(8,128)} collective-permute-done((f32[512,8,1024]{2,0,1:T(8,128)}, f32[512,8,1024]{2,0,1:T(8,128)}, u32[]{:S(2)}, u32[]{:S(2)}) %collective-permute-start) | collective-permute-done | bytes 16777248 | tf_op jit(solution)/shard_map/ppermute | solution.py:8
  551.1 15.2 %select_convert_fusion = bf16[512,8,1024]{2,0,1:T(8,128)(2,1)} fusion(f32[512,8,1024]{2,0,1:T(8,128)} %convolution_bitcast_fusion, f32[512,8,1024]{2,0,1:T(8,128)} %collective-permute-done, pred[8,1024]{1,0:T(8,128)(4,1)S(1)} %select_compare_fusion), kind=kLoop, calls=%fused_computation | loop fusion | flops 12582912 | bytes 41951232 | tf_op jit(solution)/shard_map/convert_element_type | solution.py:32
  566.3 11.5 %copy.6 = bf16[512,8,1024]{2,1,0:T(8,128)(2,1)} copy(bf16[512,8,1024]{2,0,1:T(8,128)(2,1)} %select_convert_fusion) | data formatting | bytes 16777216 | tf_op jit(solution)/shard_map/convert_element_type | solution.py:32
  (2 shorter events, 0.0 us)
Async XLA Ops:
  6.5 76.8 %all-gather.3.cloned.1.call-start = ((), (), s32[]{:S(2)}) async-start(), calls=%async_computation | async-start | bytes 8912896 | tf_op jit(solution)/shard_map/all_gather | solution.py:16
  7.3 163.1 %all-gather.5.cloned.1.call-start = ((), (), s32[]{:S(2)}) async-start(), calls=%async_computation.1 | async-start | bytes 18874368 | tf_op jit(solution)/shard_map/all_gather | solution.py:27
  8.7 181.8 %copy-start = (s32[8]{0:T(128)S(1)}, s32[8]{0:T(128)}, u32[]{:S(2)}) copy-start(s32[8]{0:T(128)} %param.7) | copy-start | bytes 100
  187.7 363.4 %collective-permute-start = (f32[512,8,1024]{2,0,1:T(8,128)}, f32[512,8,1024]{2,0,1:T(8,128)}, u32[]{:S(2)}, u32[]{:S(2)}) collective-permute-start(f32[512,8,1024]{2,0,1:T(8,128)} %convolution_bitcast_fusion), channel_id=1, source_target_pairs={{0,64},{8,72},{16,80},{24,88},{32,96},{40,104},{48,112},{56,120},{... | collective-permute-start | bytes 50331656 | tf_op jit(solution)/shard_map/ppermute | solution.py:8
Sparse Core Ops, SparseCore 0:
  9.5 73.8 all-gather.2
  85.1 85.2 all-gather.4
where the time goes:
time: 585 us
  waiting for transfers between devices  524 us (90%)
  matrix products  17.4 us (3%)
  other arithmetic  16 us (3%)
  between operations  13.4 us (2%)
  local copies, waits for them, and re-layouts  11.5 us (2%)
    ppermute x1, waiting for transfers between devices, partner(): lax.ppermute(array, axis, [(i, i ^ 1 << bit) for i in range(lax.axis_size...  361 us
    all_gather x1, waiting for transfers between devices, per_device(): lax.all_gather(integrals, 'col', axis=1, tiled=True)  87 us
    all_gather x1, waiting for transfers between devices, per_device(): amp_full = lax.all_gather(amplitudes, 'row', axis=2, tiled=True)  74.6 us
    dot_general x1, matrix products, per_device(): jnp.einsum('oik,ikn->oin', live_amps, lax.all_gather(integrals, 'col', ax...  17.4 us
    convert_element_type x1, other arithmetic, per_device(): jnp.where(keep[None], difference, jnp.zeros_like(difference))  15.2 us
  transfers between devices with their start and end apart: 3, of which 3 were waited for; matrix products, arithmetic and copies ran while one was open for 0% of the time, Pallas kernels for 0%

commit v1 on v0

v1 whole, which is shorter than its diff:
```python
import functools

import jax
import jax.numpy as jnp
from jax import lax
from jax.experimental import pallas as pl
from jax.experimental.pallas import tpu as pltpu
from jax.sharding import PartitionSpec as P

MESH = pl.DeviceIdType.MESH
IRREPS = 8
PAIRS = 4
SIDE = 4
OCC = 512
DEPTH = 128
WIDTH = 1024
NABG = 8192
TILE = 256
D_KINDS = 8
A_KINDS = 20


def ring(value, step):
    return lax.rem(value + step + SIDE, SIDE)


def kernel(
    cd_ref, ab_ref, amps_ref, ints_ref, out_ref,
    a_all, b_mine, b_other, d_all, peaks, peaks_other, rows_up, scales, a_now, staged,
    b_send, b_recv, d_send, d_recv, a_send, a_recv, s_send, s_recv, here_sem, out_sem,
):
    row, col = lax.axis_index("row"), lax.axis_index("col")
    y, x = row // SIDE, lax.rem(row, SIDE)
    z, core = col // 2, lax.rem(col, 2)
    ids = lambda yy, xx, zz, cc: (yy * SIDE + xx, zz * 2 + cc)
    across = ids(ring(y, 2), x, z, core)
    up_y, down_y = ids(ring(y, 1), x, z, core), ids(ring(y, -1), x, z, core)
    up_x, down_x = ids(y, ring(x, 1), z, core), ids(y, ring(x, -1), z, core)
    up_z, down_z = ids(y, x, ring(z, 1), core), ids(y, x, ring(z, -1), core)
    sibling = ids(y, x, z, 1 - core)
    everyone_z = [ids(y, x, ring(z, s), core) for s in (1, 2, 3)]
    everyone_z += [ids(y, x, ring(z, s), 1 - core) for s in (0, 1, 2, 3)]
    near = [across, up_y, down_y, up_x, down_x, *everyone_z]

    barrier = pltpu.get_barrier_semaphore()
    for device in near:
        pl.semaphore_signal(barrier, inc=1, device_id=device, device_id_type=MESH)
    load_a = pltpu.make_async_copy(amps_ref, a_all.at[:, row], here_sem.at[0])
    load_b = pltpu.make_async_copy(ints_ref, b_mine, here_sem.at[1])
    load_a.start()
    load_b.start()
    pl.semaphore_wait(barrier, len(near))

    def remote(source, target, send, recv, device):
        return pltpu.make_async_remote_copy(
            src_ref=source, dst_ref=target, send_sem=send, recv_sem=recv, device_id=device, device_id_type=MESH
        )

    def b_copy(g):
        return remote(ints_ref.at[g], b_other.at[g], b_send.at[g], b_recv.at[g], across)

    low, high, whole = pl.ds(0, 64), pl.ds(64, 64), pl.ds(0, DEPTH)
    slot = lambda s, c: ring(z, s) * 2 + c
    other = 1 - core
    d_kinds = [
        (slot(0, core), whole, up_z, slot(-1, core)),
        (slot(0, core), whole, down_z, slot(1, core)),
        (slot(0, core), whole, sibling, slot(0, other)),
        (slot(-1, core), low, up_z, slot(2, core)),
        (slot(1, core), high, down_z, slot(2, core)),
        (slot(-1, core), whole, sibling, slot(-1, other)),
        (slot(1, core), whole, sibling, slot(1, other)),
        (slot(2, core), whole, sibling, slot(2, other)),
    ]

    def d_copy(g, kind, arriving=False):
        leaves, rows, device, fills = d_kinds[kind]
        place = d_all.at[g, fills if arriving else leaves, rows]
        return remote(place, place, d_send.at[g, kind], d_recv.at[g, kind], device)

    first, second, every = pl.ds(0, OCC // 2), pl.ds(OCC // 2, OCC // 2), pl.ds(0, OCC)
    block = lambda sy, sx: ring(y, sy) * SIDE + ring(x, sx)
    a_kinds = [
        (block(0, 0), every, up_y, block(-1, 0)),
        (block(0, 0), every, down_y, block(1, 0)),
        (block(-1, 0), first, up_y, block(2, 0)),
        (block(1, 0), second, down_y, block(2, 0)),
    ]
    for sy in (0, -1, 1, 2):
        a_kinds += [
            (block(sy, 0), every, up_x, block(sy, -1)),
            (block(sy, 0), every, down_x, block(sy, 1)),
            (block(sy, -1), first, up_x, block(sy, 2)),
            (block(sy, 1), second, down_x, block(sy, 2)),
        ]

    def a_copy(p, kind, arriving=False):
        leaves, rows, device, fills = a_kinds[kind]
        place = a_all.at[p, fills if arriving else leaves, rows]
        return remote(place, place, a_send.at[p, kind], a_recv.at[p, kind], device)

    def s_copy(n, mine):
        return remote(scales.at[mine], scales.at[mine], s_send.at[n], s_recv.at[n], everyone_z[n])

    def a_own(p):
        for kind in (4, 5, 0, 1):
            a_copy(p, kind).start()

    def a_first(p):
        a_copy(p, 0, True).wait_recv()
        a_copy(p, 2).start()
        a_copy(p, 8).start()
        a_copy(p, 9).start()
        a_copy(p, 1, True).wait_recv()
        a_copy(p, 3).start()
        a_copy(p, 12).start()
        a_copy(p, 13).start()
        a_copy(p, 4, True).wait_recv()
        a_copy(p, 6).start()
        a_copy(p, 5, True).wait_recv()
        a_copy(p, 7).start()

    def a_next(p):
        a_copy(p, 2, True).wait_recv()
        a_copy(p, 3, True).wait_recv()
        a_copy(p, 16).start()
        a_copy(p, 17).start()
        for kind in (8, 9, 12, 13):
            a_copy(p, kind, True).wait_recv()
            a_copy(p, kind + 2).start()

    def a_last(p):
        for kind in (16, 17):
            a_copy(p, kind, True).wait_recv()
            a_copy(p, kind + 2).start()

    def a_end(p):
        for kind in (6, 7, 10, 11, 14, 15, 18, 19):
            a_copy(p, kind, True).wait_recv()

    lane = lax.broadcasted_iota(jnp.int32, (DEPTH, DEPTH), 1)
    depth_at = col * DEPTH + lax.broadcasted_iota(jnp.int32, (DEPTH, WIDTH), 0)
    place_at = lax.rem(row, SIDE * SIDE // 2) * WIDTH + lax.broadcasted_iota(jnp.int32, (DEPTH, WIDTH), 1)

    def form(g):
        b_copy(g).wait_recv()
        ups = jnp.sum(jnp.where(lane == g, rows_up[...], 0.0), axis=1, keepdims=True)
        difference = b_mine[g].astype(jnp.float32) - b_other[g].astype(jnp.float32)
        keep = (depth_at < cd_ref[g]) & (place_at < ab_ref[g])
        scaled = jnp.where(keep, difference * (ups * 32768.0), 0.0)
        whole_number = jnp.round(jnp.minimum(scaled, 32767.0)).astype(jnp.int32)
        d_all[g, col] = whole_number.astype(jnp.int16)
        for kind in (0, 1, 2):
            d_copy(g, kind).start()

    def forward(g):
        d_copy(g, 0, True).wait_recv()
        d_copy(g, 3).start()
        d_copy(g, 5).start()
        d_copy(g, 1, True).wait_recv()
        d_copy(g, 4).start()
        d_copy(g, 6).start()

    def forward_last(g):
        d_copy(g, 3, True).wait_recv()
        d_copy(g, 4, True).wait_recv()
        d_copy(g, 7).start()

    half = lax.broadcasted_iota(jnp.int32, (OCC, 128), 1) < 64

    def out_copy(g, parity):
        return pltpu.make_async_copy(staged.at[parity], out_ref.at[g], out_sem.at[parity])

    def multiply(p, parity):
        g = 2 * p + parity
        for kind in (2, 5, 6, 7):
            d_copy(g, kind, True).wait_recv()
        for m in range(8):
            left, right = a_all[p, 2 * m].astype(jnp.float32), a_all[p, 2 * m + 1].astype(jnp.float32)
            if parity == 0:
                joined = jnp.where(half, left, pltpu.roll(right, 64, 1))
            else:
                joined = jnp.where(half, pltpu.roll(left, 64, 1), right)
            scaled = joined * scales[m, pl.ds(g, 1), :]
            a_now[:, m * 128 : (m + 1) * 128] = scaled.astype(jnp.bfloat16)

        @pl.when(p > 0)
        def _():
            out_copy(g, parity).wait()

        def columns(n, _):
            at = pl.ds(pl.multiple_of(n * TILE, TILE), TILE)
            d = d_all[g, :, :, at].reshape(8 * DEPTH, TILE).astype(jnp.float32)
            top = d.astype(jnp.bfloat16)
            rest = (d - top.astype(jnp.float32)).astype(jnp.bfloat16)
            total = jnp.dot(a_now[...], top, preferred_element_type=jnp.float32)
            total += jnp.dot(a_now[...], rest, preferred_element_type=jnp.float32)
            staged[parity, :, at] = (total * (1.0 / 32768.0)).astype(jnp.bfloat16)
            return 0

        lax.fori_loop(0, WIDTH // TILE, columns, 0)
        out_copy(g, parity).start()

    b_copy(0).start()
    load_a.wait()
    a_copy(0, 4).start()
    a_copy(0, 5).start()
    load_b.wait()

    def peak(g, _):
        size = jnp.abs(b_mine[g].astype(jnp.float32))
        size = jnp.where(place_at < ab_ref[g], size, 0.0)
        most = jnp.max(size, axis=1, keepdims=True)
        peaks[pl.ds(g, 1), :] = jnp.transpose(jnp.broadcast_to(most, (DEPTH, DEPTH)))[0:1, :]
        return 0

    lax.fori_loop(0, IRREPS, peak, 0)
    peak_copy = remote(peaks, peaks_other, s_send.at[7], s_recv.at[7], across)
    peak_copy.start()
    b_copy(1).start()
    a_copy(0, 0).start()
    a_copy(0, 1).start()
    peak_copy.wait_recv()
    left = peaks[...] + peaks_other[...]
    up, down = jnp.ones_like(left), jnp.ones_like(left)
    for power in (32, 16, 8, 4, 2, 1):
        small = left < 2.0**-power
        left = jnp.where(small, left * 2.0**power, left)
        up = jnp.where(small, up * 2.0**power, up)
        down = jnp.where(small, down * 2.0**-power, down)
    rows_up[...] = jnp.transpose(jnp.concatenate([up] * 16, axis=0))
    scales[col] = down
    for n in range(7):
        s_copy(n, col).start()

    def step(p, _):
        for parity in (0, 1):
            g = 2 * p + parity

            @pl.when(g + 2 < IRREPS)
            def _():
                b_copy(g + 2).start()

            @pl.when(g < IRREPS)
            def _():
                form(g)

            if parity == 0:
                @pl.when(p + 1 < PAIRS)
                def _():
                    a_own(p + 1)

                @pl.when(p < PAIRS)
                def _():
                    a_first(p)

                @pl.when((p >= 1) & (p <= PAIRS))
                def _():
                    a_last(p - 1)
            else:
                @pl.when(p < PAIRS)
                def _():
                    a_next(p)

            @pl.when((g >= 1) & (g <= IRREPS))
            def _():
                forward(g - 1)

            @pl.when((g >= 2) & (g <= IRREPS + 1))
            def _():
                forward_last(g - 2)

            if parity == 1:
                @pl.when((p >= 1) & (p <= PAIRS))
                def _():
                    a_end(p - 1)

            @pl.when((g >= 3) & (g <= IRREPS + 2))
            def _():
                multiply((g - 3) // 2, 1 - parity)
        return 0

    step(0, 0)
    for n in range(7):
        sender = [slot(-1, core), slot(-2, core), slot(-3, core)] + [slot(-s, other) for s in (0, 1, 2, 3)]
        s_copy(n, sender[n]).wait_recv()
    lax.fori_loop(1, PAIRS + 2, step, 0)

    for parity in (0, 1):
        out_copy(0, parity).wait()
    for n in range(7):
        s_copy(n, col).wait_send()
    peak_copy.wait_send()

    def drain_b(g, _):
        b_copy(g).wait_send()
        for kind in range(D_KINDS):
            d_copy(g, kind).wait_send()
        return 0

    def drain_a(p, _):
        for kind in range(A_KINDS):
            a_copy(p, kind).wait_send()
        return 0

    lax.fori_loop(0, IRREPS, drain_b, 0)
    lax.fori_loop(0, PAIRS, drain_a, 0)


def per_device(amplitudes, integrals, cd_count, ab_count):
    pairs = amplitudes.reshape(OCC, PAIRS, 128).transpose(1, 0, 2)
    ladder = pl.pallas_call(
        kernel,
        out_shape=jax.ShapeDtypeStruct((IRREPS, OCC, WIDTH), jnp.bfloat16),
        in_specs=[
            pl.BlockSpec(memory_space=pltpu.SMEM),
            pl.BlockSpec(memory_space=pltpu.SMEM),
            pl.BlockSpec(memory_space=pl.ANY),
            pl.BlockSpec(memory_space=pl.ANY),
        ],
        out_specs=pl.BlockSpec(memory_space=pl.ANY),
        scratch_shapes=[
            pltpu.VMEM((PAIRS, 16, OCC, 128), jnp.bfloat16),
            pltpu.VMEM((IRREPS, DEPTH, WIDTH), jnp.bfloat16),
            pltpu.VMEM((IRREPS, DEPTH, WIDTH), jnp.bfloat16),
            pltpu.VMEM((IRREPS, 8, DEPTH, WIDTH), jnp.int16),
            pltpu.VMEM((IRREPS, DEPTH), jnp.float32),
            pltpu.VMEM((IRREPS, DEPTH), jnp.float32),
            pltpu.VMEM((DEPTH, DEPTH), jnp.float32),
            pltpu.VMEM((8, IRREPS, DEPTH), jnp.float32),
            pltpu.VMEM((OCC, 8 * DEPTH), jnp.bfloat16),
            pltpu.VMEM((2, OCC, WIDTH), jnp.bfloat16),
            pltpu.SemaphoreType.DMA((IRREPS,)),
            pltpu.SemaphoreType.DMA((IRREPS,)),
            pltpu.SemaphoreType.DMA((IRREPS, D_KINDS)),
            pltpu.SemaphoreType.DMA((IRREPS, D_KINDS)),
            pltpu.SemaphoreType.DMA((PAIRS, A_KINDS)),
            pltpu.SemaphoreType.DMA((PAIRS, A_KINDS)),
            pltpu.SemaphoreType.DMA((8,)),
            pltpu.SemaphoreType.DMA((8,)),
            pltpu.SemaphoreType.DMA((2,)),
            pltpu.SemaphoreType.DMA((2,)),
        ],
        compiler_params=pltpu.CompilerParams(
            collective_id=0, has_side_effects=True, vmem_limit_bytes=52 << 20
        ),
        cost_estimate=pl.CostEstimate(flops=17 << 30, bytes_accessed=12 << 20, transcendentals=0),
    )(cd_count, ab_count, pairs, integrals)
    return ladder.transpose(1, 0, 2)


def solution(mesh):
    in_specs = (P("col", None, "row"), P(None, "col", "row"), P(), P())
    out_specs = P("col", None, "row")
    return jax.shard_map(
        per_device, mesh=mesh, in_specs=in_specs, out_specs=out_specs, check_vma=False
    )
```

time: 585 us -> 124 us (0.21)
  waiting for transfers between devices: 524 us -> 0 us
  Pallas kernels: 0 us -> 109 us
  matrix products: 17.4 us -> 0 us
  other arithmetic: 16 us -> 0 us
  between operations: 13.4 us -> 0.03 us
    ppermute x1 -> x0, waiting for transfers between devices: 361 us -> none  [partner(): lax.ppermute(array, axis, [(i, i ^ 1 << bit) for i in range(lax.axis_size...]
    all_gather x2 -> x0, waiting for transfers between devices: 162 us -> none  [the longest x1 87 us: per_device(): lax.all_gather(integrals, 'col', axis=1, tiled=True)]
    pallas_call x0 -> x1, Pallas kernels: none -> 109 us  [per_device(): pl.pallas_call(kernel, out_shape=jax.ShapeDtypeStruct((IRREPS, OCC, WIDTH...]
    dot_general x1 -> x0, matrix products: 17.4 us -> none  [per_device(): jnp.einsum('oik,ikn->oin', live_amps, lax.all_gather(integrals, 'col', ax...]
    convert_element_type x1 -> x0, other arithmetic: 15.2 us -> none  [per_device(): jnp.where(keep[None], difference, jnp.zeros_like(difference))]
    transpose x0 -> x1, local copies, waits for them, and re-layouts: none -> 11.5 us  [per_device(): return ladder.transpose(1, 0, 2)]
    convert_element_type x1 -> x0, local copies, waits for them, and re-layouts: 11.5 us -> none  [per_device(): jnp.where(keep[None], difference, jnp.zeros_like(difference))]
  transfers between devices with their start and end apart: 3 -> 0, of which waited for: 3 -> 0; matrix products, arithmetic and copies ran while one was open for 0% -> 0% of each run, Pallas kernels for 0% -> 0%
where the time goes in v1:
time: 124 us; the launch traced here: 123 us
  Pallas kernels  109 us (88%)
  local copies, waits for them, and re-layouts  14.1 us (11%)
    pallas_call x1, Pallas kernels, per_device(): pl.pallas_call(kernel, out_shape=jax.ShapeDtypeStruct((IRREPS, OCC, WIDTH...  109 us
    transpose x1, local copies, waits for them, and re-layouts, per_device(): return ladder.transpose(1, 0, 2)  11.5 us

profile of v1, /device:TPU:1, one launch (start us, length us, event | category | flops | bytes accessed | tf_op | source)
XLA Modules:
  0.0 122.8 jit_solution(6897233823938520558)
XLA Ops:
  0.0 1.3 %copy.6 = bf16[512,4,128]{2,0,1:T(8,128)(2,1)S(1)} copy(bf16[512,4,128]{0,2,1:T(8,128)(2,1)} %bitcast.5) | data formatting | bytes 1048576 | tf_op jit(solution)/shard_map/reshape | solution.py:311
  1.3 0.0 copy-start
  1.3 0.6 copy-done
  2.0 0.0 copy-start.1
  2.0 0.7 copy-done.1
  2.6 108.7 %shard_map.46 = bf16[8,512,1024]{2,1,0:T(8,128)(2,1)} custom-call(s32[8]{0:T(128)S(1)} %copy-done, s32[8]{0:T(128)S(1)} %copy-done.1, bf16[4,512,128]{2,1,0:T(8,128)(2,1)S(1)} %bitcast.3, bf16[8,128,1024]{2,1,0:T(8,128)(2,1)} %ints_ref.1), custom_call_target="tpu_custom_call" | custom-call | flops 18253611008 | bytes 12582912 | tf_op jit(solution)/shard_map/pallas_call | solution.py:312
  111.3 11.5 %copy.7 = bf16[512,8,1024]{2,1,0:T(8,128)(2,1)} copy(bf16[512,8,1024]{2,0,1:T(8,128)(2,1)} %bitcast.4) | data formatting | bytes 16777216 | tf_op jit(solution)/shard_map/transpose | solution.py:349
Async XLA Ops:
  1.3 0.7 copy-start
  2.0 0.7 copy-start.1

commit v2 on v0

v2 whole, which is shorter than its diff:
```python
import functools

import jax
import jax.numpy as jnp
from jax import lax
from jax.experimental import pallas as pl
from jax.experimental.pallas import tpu as pltpu
from jax.sharding import PartitionSpec as P

MESH = pl.DeviceIdType.MESH
IRREPS = 8
PAIRS = 4
SIDE = 4
OCC = 512
DEPTH = 128
WIDTH = 1024
NABG = 8192
TILE = 256
D_KINDS = 10
A_KINDS = 20
UNITS = 36
STRIPS = 4
SLAB = 32
GROUP = 2 * DEPTH

PLAN = {
    0: [
        ("own_x", 1), ("own_x", 2), ("send_b", 1), ("on_x", 0, 4), ("on_x", 0, 5),
        ("form", 0, 0), ("on_x", 1, 4), ("on_x", 1, 5), ("form", 0, 1), ("own_x", 3),
        ("own_y", 1), ("up_y", 0), ("down_y", 0), ("on_x", 2, 4), ("on_x", 2, 5),
        ("up_z", 0), ("send_b", 2), ("form", 1, 0), ("share_up", 0), ("down_z", 0),
        ("share_down", 0), ("on_x", 3, 4), ("on_x", 3, 5), ("form", 1, 1), ("up_y", 1),
        ("down_y", 1), ("on_x", 0, 8), ("on_x", 0, 9), ("up_z", 1), ("far_y", 0),
        ("send_b", 3), ("on_x", 0, 12), ("on_x", 0, 13), ("share_up", 1), ("share_far", 0),
        ("form", 2, 0), ("down_z", 1), ("share_down", 1), ("own_y", 2), ("form", 2, 1),
        ("far_y", 1), ("on_x", 1, 8), ("on_x", 1, 9), ("send_b", 4), ("up_z", 2),
        ("on_x", 1, 12), ("on_x", 1, 13), ("form", 3, 0), ("share_up", 2), ("share_far", 1),
        ("form", 3, 1), ("on_x", 0, 16), ("on_x", 0, 17), ("send_b", 5), ("down_z", 2),
        ("share_down", 2), ("up_y", 2), ("down_y", 2), ("up_z", 3), ("on_x", 1, 16),
        ("on_x", 1, 17), ("form", 4, 0), ("share_up", 3), ("down_z", 3), ("share_down", 3),
        ("own_y", 3), ("form", 4, 1),
    ],
    1: [
        ("share_far", 2),
    ],
    2: [
        ("form", 5, 0), ("on_x", 2, 8), ("on_x", 2, 9), ("send_b", 6),
    ],
    3: [
        ("up_z", 4),
    ],
    4: [
        ("form", 5, 1), ("far_y", 2), ("on_x", 2, 12), ("on_x", 2, 13),
    ],
    5: [
        ("share_up", 4), ("share_far", 3), ("send_b", 7),
    ],
    6: [
        ("up_y", 3), ("down_y", 3), ("up_z", 5), ("down_z", 4), ("share_down", 4),
    ],
    8: [
        ("on_x", 2, 16), ("on_x", 2, 17),
    ],
    9: [
        ("form", 6, 0),
    ],
    11: [
        ("form", 6, 1), ("share_up", 5), ("down_z", 5), ("share_down", 5), ("on_x", 3, 8),
        ("on_x", 3, 9),
    ],
    13: [
        ("form", 7, 0), ("share_far", 4), ("on_x", 3, 12), ("on_x", 3, 13),
    ],
    14: [
        ("form", 7, 1), ("up_z", 6),
    ],
    15: [
        ("far_y", 3),
    ],
    17: [
        ("share_up", 6), ("down_z", 6), ("share_down", 6),
    ],
    19: [
        ("up_z", 7), ("share_far", 5),
    ],
    20: [
        ("on_x", 3, 16), ("on_x", 3, 17), ("share_up", 7),
    ],
    22: [
        ("down_z", 7), ("share_down", 7),
    ],
    24: [
        ("share_far", 6),
    ],
    25: [
        ("share_far", 7),
    ],
}


def ring(value, step):
    return lax.rem(value + step + SIDE, SIDE)


def kernel(
    cd_hbm, ab_hbm, amps_ref, ints_ref, out_ref,
    cd_ref, ab_ref, a_mine, a_all, b_mine, b_other, d_all, peaks, peaks_other, rows_up, scales, a_now, partial, staged,
    b_send, b_recv, d_send, d_recv, a_send, a_recv, s_send, s_recv, here_sem, out_sem,
):
    row, col = lax.axis_index("row"), lax.axis_index("col")
    y, x = row // SIDE, lax.rem(row, SIDE)
    z, core = col // 2, lax.rem(col, 2)
    other = 1 - core
    ids = lambda yy, xx, zz, cc: (yy * SIDE + xx, zz * 2 + cc)
    across = ids(ring(y, 2), x, z, core)
    up_y, down_y = ids(ring(y, 1), x, z, core), ids(ring(y, -1), x, z, core)
    up_x, down_x = ids(y, ring(x, 1), z, core), ids(y, ring(x, -1), z, core)
    up_z, down_z = ids(y, x, ring(z, 1), core), ids(y, x, ring(z, -1), core)
    sibling = ids(y, x, z, other)
    everyone_z = [ids(y, x, ring(z, s), core) for s in (1, 2, 3)]
    everyone_z += [ids(y, x, ring(z, s), other) for s in (0, 1, 2, 3)]
    near = [across, up_y, down_y, up_x, down_x, *everyone_z]

    barrier = pltpu.get_barrier_semaphore()
    for device in near:
        pl.semaphore_signal(barrier, inc=1, device_id=device, device_id_type=MESH)
    loads = [
        pltpu.make_async_copy(source, target, here_sem.at[n])
        for n, (source, target) in enumerate(
            ((amps_ref, a_mine), (ab_hbm, ab_ref), (cd_hbm, cd_ref), (ints_ref, b_mine))
        )
    ]
    for load in loads:
        load.start()

    def remote(source, target, send, recv, device):
        return pltpu.make_async_remote_copy(
            src_ref=source, dst_ref=target, send_sem=send, recv_sem=recv, device_id=device, device_id_type=MESH
        )

    low, high, whole = pl.ds(0, DEPTH // 2), pl.ds(DEPTH // 2, DEPTH // 2), pl.ds(0, DEPTH)
    halves = (low, high)

    def b_copy(g, h):
        return remote(
            ints_ref.at[g, halves[h]], b_other.at[g, halves[h]], b_send.at[g, h], b_recv.at[g, h], across
        )

    slot = lambda s, c: ring(z, s) * 2 + c
    d_kinds = [
        (slot(0, core), low, up_z, slot(-1, core)),
        (slot(0, core), high, up_z, slot(-1, core)),
        (slot(0, core), low, down_z, slot(1, core)),
        (slot(0, core), high, down_z, slot(1, core)),
        (slot(-1, core), low, up_z, slot(2, core)),
        (slot(1, core), high, down_z, slot(2, core)),
        (slot(0, core), whole, sibling, slot(0, other)),
        (slot(-1, core), whole, sibling, slot(-1, other)),
        (slot(1, core), whole, sibling, slot(1, other)),
        (slot(2, core), whole, sibling, slot(2, other)),
    ]

    def d_copy(g, kind, arriving=False):
        leaves, rows, device, fills = d_kinds[kind]
        place = d_all.at[g, fills if arriving else leaves, rows]
        return remote(place, place, d_send.at[g, kind], d_recv.at[g, kind], device)

    first, second, every = pl.ds(0, OCC // 2), pl.ds(OCC // 2, OCC // 2), pl.ds(0, OCC)
    block = lambda sy, sx: ring(y, sy) * SIDE + ring(x, sx)
    a_kinds = [
        (block(0, 0), every, up_y, block(-1, 0)),
        (block(0, 0), every, down_y, block(1, 0)),
        (block(-1, 0), first, up_y, block(2, 0)),
        (block(1, 0), second, down_y, block(2, 0)),
    ]
    for sy in (0, -1, 1, 2):
        a_kinds += [
            (block(sy, 0), every, up_x, block(sy, -1)),
            (block(sy, 0), every, down_x, block(sy, 1)),
            (block(sy, -1), first, up_x, block(sy, 2)),
            (block(sy, 1), second, down_x, block(sy, 2)),
        ]

    def a_copy(p, kind, arriving=False):
        leaves, rows, device, fills = a_kinds[kind]
        place = a_all.at[p, fills if arriving else leaves, rows]
        return remote(place, place, a_send.at[p, kind], a_recv.at[p, kind], device)

    def s_copy(n, mine):
        return remote(scales.at[mine], scales.at[mine], s_send.at[n], s_recv.at[n], everyone_z[n])

    def send_b(g):
        b_copy(g, 0).start()
        b_copy(g, 1).start()

    def moves(p, waits, starts):
        for kind in waits:
            a_copy(p, kind, True).wait_recv()
        for kind in starts:
            a_copy(p, kind).start()

    def passes(g, waits, kind):
        for arrived in waits:
            d_copy(g, arrived, True).wait_recv()
        d_copy(g, kind).start()

    lane = lax.broadcasted_iota(jnp.int32, (DEPTH // 2, DEPTH), 1)
    depth_at = col * DEPTH + lax.broadcasted_iota(jnp.int32, (DEPTH // 2, WIDTH), 0)
    place_at = lax.rem(row, SIDE * SIDE // 2) * WIDTH + lax.broadcasted_iota(jnp.int32, (DEPTH // 2, WIDTH), 1)

    def form(g, h):
        ups = jnp.sum(jnp.where(lane == g, rows_up[halves[h], :], 0.0), axis=1, keepdims=True) * 32768.0
        b_copy(g, h).wait_recv()
        mine, theirs = b_mine[g, halves[h], :], b_other[g, halves[h], :]
        difference = mine.astype(jnp.float32) - theirs.astype(jnp.float32)
        keep = (depth_at < cd_ref[g] - h * (DEPTH // 2)) & (place_at < ab_ref[g])
        scaled = jnp.where(keep, difference * ups, 0.0)
        whole_number = jnp.round(jnp.minimum(scaled, 32767.0)).astype(jnp.int32)
        d_all[g, col, halves[h], :] = whole_number.astype(jnp.int16)
        d_copy(g, h).start()
        d_copy(g, 2 + h).start()
        if h == 1:
            d_copy(g, 6).start()

    does = {
        "form": form,
        "send_b": send_b,
        "own_x": lambda p: moves(p, (), (4, 5)),
        "own_y": lambda p: moves(p, (), (0, 1)),
        "up_y": lambda p: moves(p, (0,), (2, 8, 9)),
        "down_y": lambda p: moves(p, (1,), (3, 12, 13)),
        "far_y": lambda p: moves(p, (2, 3), (16, 17)),
        "on_x": lambda p, kind: moves(p, (kind,), (kind + 2,)),
        "up_z": lambda g: passes(g, (0,), 4),
        "down_z": lambda g: passes(g, (3,), 5),
        "share_up": lambda g: passes(g, (1,), 7),
        "share_down": lambda g: passes(g, (2,), 8),
        "share_far": lambda g: passes(g, (4, 5), 9),
    }

    half = lax.broadcasted_iota(jnp.int32, (OCC, DEPTH), 1) < DEPTH // 2
    chips = (0, -1, 1, 2)

    def product(g, groups, at):
        d = jnp.concatenate(
            [d_all[g, pl.ds(2 * ring(z, chips[i]), 2), :, at].reshape(GROUP, TILE) for i in groups], axis=0
        ).astype(jnp.float32)
        top = d.astype(jnp.bfloat16)
        rest = (d - top.astype(jnp.float32)).astype(jnp.bfloat16)
        a = a_now[:, groups[0] * GROUP : (groups[-1] + 1) * GROUP]
        summed = jnp.dot(a, top, preferred_element_type=jnp.float32)
        summed += jnp.dot(a, rest, preferred_element_type=jnp.float32)
        return summed * (1.0 / 32768.0)

    def gather(g):
        p, parity = g // 2, lax.rem(g, 2)

        @pl.when(parity == 0)
        def _():
            for kind in (6, 7, 10, 11, 14, 15, 18, 19):
                a_copy(p, kind, True).wait_recv()

        for kind in (6, 7, 8):
            d_copy(g, kind, True).wait_recv()
        for i in range(SIDE):
            for c in (0, 1):
                m = 2 * ring(z, chips[i]) + c
                left = pltpu.roll(a_all[p, 2 * m].astype(jnp.float32), 64 * parity, 1)
                right = pltpu.roll(a_all[p, 2 * m + 1].astype(jnp.float32), 64 - 64 * parity, 1)
                joined = jnp.where(half, left, right) * scales[m, pl.ds(g, 1), :]
                k = (2 * i + c) * DEPTH
                a_now[:, k : k + DEPTH] = joined.astype(jnp.bfloat16)

    def strip(n):
        return pl.ds(pl.multiple_of(n * TILE, TILE), TILE)

    def out_copy(g, n):
        parity = lax.rem(g, 2)
        return pltpu.make_async_copy(
            staged.at[parity, n], out_ref.at[g, :, strip(n)], out_sem.at[parity, n]
        )

    def multiply_most(g, n):
        partial[n] = product(g, (0, 1, 2), strip(n))

    def multiply_rest(g, n):
        pl.when(g >= 2)(lambda: out_copy(g - 2, n).wait())
        staged[lax.rem(g, 2), n] = (partial[n] + product(g, (3,), strip(n))).astype(jnp.bfloat16)
        out_copy(g, n).start()

    for load in loads[1:]:
        load.wait()

    def peak(g, _):
        most = []
        for h in (0, 1):
            size = jnp.abs(b_mine[g, halves[h], :].astype(jnp.float32))
            size = jnp.where(place_at < ab_ref[g], size, 0.0)
            most.append(jnp.max(size, axis=1, keepdims=True))
        spread = jnp.broadcast_to(jnp.concatenate(most, axis=0), (DEPTH, DEPTH))
        peaks[pl.ds(g, 1), :] = jnp.transpose(spread)[0:1, :]
        return 0

    lax.fori_loop(0, IRREPS, peak, 0)
    pl.semaphore_wait(barrier, len(near))
    peak_copy = remote(peaks, peaks_other, s_send.at[7], s_recv.at[7], across)
    peak_copy.start()
    send_b(0)
    loads[0].wait()
    for p in range(PAIRS):
        a_all[p, row] = jnp.transpose(a_mine[p].astype(jnp.float32)).astype(jnp.bfloat16)
        if p == 0:
            moves(0, (), (4, 5, 0, 1))
    peak_copy.wait_recv()
    left = peaks[...] + peaks_other[...]
    up, down = jnp.ones_like(left), jnp.ones_like(left)
    for power in (32, 16, 8, 4, 2, 1):
        small = left < 2.0**-power
        left = jnp.where(small, left * 2.0**power, left)
        up = jnp.where(small, up * 2.0**power, up)
        down = jnp.where(small, down * 2.0**-power, down)
    rows_up[...] = jnp.transpose(jnp.concatenate([up] * 16, axis=0))
    scales[col] = down
    for n in range(7):
        s_copy(n, col).start()

    def unit(i, _):
        for at, calls in PLAN.items():
            @pl.when(i == at)
            def _(calls=calls):
                for name, *where in calls:
                    does[name](*where)

        @pl.when(i == 0)
        def _():
            sender = [slot(-1, core), slot(-2, core), slot(-3, core)] + [slot(-n, other) for n in (0, 1, 2, 3)]
            for n in range(7):
                s_copy(n, sender[n]).wait_recv()

        g, n = i // STRIPS, lax.rem(i, STRIPS)
        last = IRREPS * STRIPS

        @pl.when(i < last)
        def _():
            pl.when(n == 0)(lambda: gather(g))
            multiply_most(g, n)

        @pl.when((i < last - STRIPS) | (i >= last))
        def _():
            block = g - i // last
            pl.when(n == 0)(lambda: d_copy(block, 9, True).wait_recv())
            multiply_rest(block, n)

        return 0

    lax.fori_loop(0, UNITS, unit, 0)

    for n in range(7):
        s_copy(n, col).wait_send()
    peak_copy.wait_send()

    def drain_b(g, _):
        b_copy(g, 0).wait_send()
        b_copy(g, 1).wait_send()
        for kind in range(D_KINDS):
            d_copy(g, kind).wait_send()
        return 0

    def drain_a(p, _):
        for kind in range(A_KINDS):
            a_copy(p, kind).wait_send()
        return 0

    lax.fori_loop(0, IRREPS, drain_b, 0)
    lax.fori_loop(0, PAIRS, drain_a, 0)
    for n in range(STRIPS):
        out_copy(IRREPS - 2, n).wait()
        out_copy(IRREPS - 1, n).wait()


def interleave(in_ref, out_ref, taken, given, in_sem, out_sem):
    def take(n):
        return pltpu.make_async_copy(in_ref.at[:, pl.ds(n * SLAB, SLAB), :], taken.at[n], in_sem.at[n])

    def give(n):
        rows = pl.ds(pl.multiple_of(n * (SLAB * IRREPS), SLAB * IRREPS), SLAB * IRREPS)
        return pltpu.make_async_copy(given.at[n], out_ref.at[rows], out_sem.at[n])

    slabs = OCC // SLAB
    for n in range(slabs):
        take(n).start()

    def slab(n, _):
        take(n).wait()
        given[n] = jnp.swapaxes(taken[n], 0, 1).reshape(SLAB * IRREPS, WIDTH)
        give(n).start()
        return 0

    lax.fori_loop(0, slabs, slab, 0)
    for n in range(slabs):
        give(n).wait()


def per_device(amplitudes, integrals, cd_count, ab_count):
    pairs = amplitudes.transpose(1, 2, 0).reshape(PAIRS, DEPTH, OCC)
    by_irrep = pl.pallas_call(
        kernel,
        out_shape=jax.ShapeDtypeStruct((IRREPS, OCC, WIDTH), jnp.bfloat16),
        in_specs=[pl.BlockSpec(memory_space=pl.ANY)] * 4,
        out_specs=pl.BlockSpec(memory_space=pl.ANY),
        scratch_shapes=[
            pltpu.SMEM((IRREPS,), jnp.int32),
            pltpu.SMEM((IRREPS,), jnp.int32),
            pltpu.VMEM((PAIRS, DEPTH, OCC), jnp.bfloat16),
            pltpu.VMEM((PAIRS, 16, OCC, DEPTH), jnp.bfloat16),
            pltpu.VMEM((IRREPS, DEPTH, WIDTH), jnp.bfloat16),
            pltpu.VMEM((IRREPS, DEPTH, WIDTH), jnp.bfloat16),
            pltpu.VMEM((IRREPS, 8, DEPTH, WIDTH), jnp.int16),
            pltpu.VMEM((IRREPS, DEPTH), jnp.float32),
            pltpu.VMEM((IRREPS, DEPTH), jnp.float32),
            pltpu.VMEM((DEPTH, DEPTH), jnp.float32),
            pltpu.VMEM((8, IRREPS, DEPTH), jnp.float32),
            pltpu.VMEM((OCC, 8 * DEPTH), jnp.bfloat16),
            pltpu.VMEM((STRIPS, OCC, TILE), jnp.float32),
            pltpu.VMEM((2, STRIPS, OCC, TILE), jnp.bfloat16),
            pltpu.SemaphoreType.DMA((IRREPS, 2)),
            pltpu.SemaphoreType.DMA((IRREPS, 2)),
            pltpu.SemaphoreType.DMA((IRREPS, D_KINDS)),
            pltpu.SemaphoreType.DMA((IRREPS, D_KINDS)),
            pltpu.SemaphoreType.DMA((PAIRS, A_KINDS)),
            pltpu.SemaphoreType.DMA((PAIRS, A_KINDS)),
            pltpu.SemaphoreType.DMA((8,)),
            pltpu.SemaphoreType.DMA((8,)),
            pltpu.SemaphoreType.DMA((4,)),
            pltpu.SemaphoreType.DMA((2, STRIPS)),
        ],
        compiler_params=pltpu.CompilerParams(
            collective_id=0, has_side_effects=True, vmem_limit_bytes=60 << 20
        ),
        cost_estimate=pl.CostEstimate(flops=17 << 30, bytes_accessed=12 << 20, transcendentals=0),
    )(cd_count, ab_count, pairs, integrals)
    slabs = OCC // SLAB
    ladder = pl.pallas_call(
        interleave,
        out_shape=jax.ShapeDtypeStruct((OCC * IRREPS, WIDTH), jnp.bfloat16),
        in_specs=[pl.BlockSpec(memory_space=pl.ANY)],
        out_specs=pl.BlockSpec(memory_space=pl.ANY),
        scratch_shapes=[
            pltpu.VMEM((slabs, IRREPS, SLAB, WIDTH), jnp.bfloat16),
            pltpu.VMEM((slabs, SLAB * IRREPS, WIDTH), jnp.bfloat16),
            pltpu.SemaphoreType.DMA((slabs,)),
            pltpu.SemaphoreType.DMA((slabs,)),
        ],
        compiler_params=pltpu.CompilerParams(vmem_limit_bytes=60 << 20),
    )(by_irrep)
    return ladder.reshape(OCC, IRREPS, WIDTH)


def solution(mesh):
    in_specs = (P("col", None, "row"), P(None, "col", "row"), P(), P())
    out_specs = P("col", None, "row")
    return jax.shard_map(
        per_device, mesh=mesh, in_specs=in_specs, out_specs=out_specs, check_vma=False
    )
```

time: 585 us -> 113 us (0.19)
  waiting for transfers between devices: 524 us -> 0 us
  Pallas kernels: 0 us -> 113 us
  matrix products: 17.4 us -> 0 us
  other arithmetic: 16 us -> 0 us
  between operations: 13.4 us -> 0.01 us
  local copies, waits for them, and re-layouts: 11.5 us -> 0 us
    ppermute x1 -> x0, waiting for transfers between devices: 361 us -> none  [partner(): lax.ppermute(array, axis, [(i, i ^ 1 << bit) for i in range(lax.axis_size...]
    all_gather x2 -> x0, waiting for transfers between devices: 162 us -> none  [the longest x1 87 us: per_device(): lax.all_gather(integrals, 'col', axis=1, tiled=True)]
    pallas_call x0 -> x2, Pallas kernels: none -> 113 us  [the longest x1 106 us: per_device(): pl.pallas_call(kernel, out_shape=jax.ShapeDtypeStruct((IRREPS, OCC, WIDTH...]
    dot_general x1 -> x0, matrix products: 17.4 us -> none  [per_device(): jnp.einsum('oik,ikn->oin', live_amps, lax.all_gather(integrals, 'col', ax...]
    convert_element_type x1 -> x0, other arithmetic: 15.2 us -> none  [per_device(): jnp.where(keep[None], difference, jnp.zeros_like(difference))]
    convert_element_type x1 -> x0, local copies, waits for them, and re-layouts: 11.5 us -> none  [per_device(): jnp.where(keep[None], difference, jnp.zeros_like(difference))]
  transfers between devices with their start and end apart: 3 -> 0, of which waited for: 3 -> 0; matrix products, arithmetic and copies ran while one was open for 0% -> 0% of each run, Pallas kernels for 0% -> 0%
where the time goes in v2:
time: 113 us
  Pallas kernels  113 us (100%)
    pallas_call x1, Pallas kernels, per_device(): pl.pallas_call(kernel, out_shape=jax.ShapeDtypeStruct((IRREPS, OCC, WIDTH...  106 us
    pallas_call x1, Pallas kernels, per_device(): pl.pallas_call(interleave, out_shape=jax.ShapeDtypeStruct((OCC * IRREPS,...  6.62 us

profile of v2, /device:TPU:1, one launch (start us, length us, event | category | flops | bytes accessed | tf_op | source)
XLA Modules:
  0.0 112.7 jit_solution(8779103495451061915)
XLA Ops:
  0.0 106.1 %shard_map.46.in_ref = bf16[8,512,1024]{2,1,0:T(8,128)(2,1)} custom-call(s32[8]{0:T(128)} %cd_hbm.1, s32[8]{0:T(128)} %ab_hbm.1, bf16[4,128,512]{2,1,0:T(8,128)(2,1)} %bitcast.4, bf16[8,128,1024]{2,1,0:T(8,128)(2,1)} %ints_ref.1), custom_call_target="tpu_custom_call" | custom-call | flops 18253611008 | bytes 12582912 | tf_op jit(solution)/shard_map/pallas_call | solution.py:406
  106.1 6.6 %shard_map.47 = bf16[4096,1024]{1,0:T(8,128)(2,1)} custom-call(bf16[8,512,1024]{2,1,0:T(8,128)(2,1)} %shard_map.46.in_ref), custom_call_target="tpu_custom_call" | custom-call | tf_op jit(solution)/shard_map/pallas_call | solution.py:443

commit v3 on v2

--- a/solution.py
+++ b/solution.py
@@ -15,84 +15,55 @@
 DEPTH = 128
 WIDTH = 1024
 NABG = 8192
-TILE = 256
+TILE = 1024
 D_KINDS = 10
 A_KINDS = 20
-UNITS = 36
-STRIPS = 4
+UNITS = 9
+STRIPS = 1
 SLAB = 32
 GROUP = 2 * DEPTH
 
 PLAN = {
     0: [
-        ("own_x", 1), ("own_x", 2), ("send_b", 1), ("on_x", 0, 4), ("on_x", 0, 5),
-        ("form", 0, 0), ("on_x", 1, 4), ("on_x", 1, 5), ("form", 0, 1), ("own_x", 3),
-        ("own_y", 1), ("up_y", 0), ("down_y", 0), ("on_x", 2, 4), ("on_x", 2, 5),
-        ("up_z", 0), ("send_b", 2), ("form", 1, 0), ("share_up", 0), ("down_z", 0),
-        ("share_down", 0), ("on_x", 3, 4), ("on_x", 3, 5), ("form", 1, 1), ("up_y", 1),
-        ("down_y", 1), ("on_x", 0, 8), ("on_x", 0, 9), ("up_z", 1), ("far_y", 0),
-        ("send_b", 3), ("on_x", 0, 12), ("on_x", 0, 13), ("share_up", 1), ("share_far", 0),
-        ("form", 2, 0), ("down_z", 1), ("share_down", 1), ("own_y", 2), ("form", 2, 1),
-        ("far_y", 1), ("on_x", 1, 8), ("on_x", 1, 9), ("send_b", 4), ("up_z", 2),
-        ("on_x", 1, 12), ("on_x", 1, 13), ("form", 3, 0), ("share_up", 2), ("share_far", 1),
-        ("form", 3, 1), ("on_x", 0, 16), ("on_x", 0, 17), ("send_b", 5), ("down_z", 2),
-        ("share_down", 2), ("up_y", 2), ("down_y", 2), ("up_z", 3), ("on_x", 1, 16),
-        ("on_x", 1, 17), ("form", 4, 0), ("share_up", 3), ("down_z", 3), ("share_down", 3),
-        ("own_y", 3), ("form", 4, 1),
+        ("own_x", 1), ("send_b", 1), ("own_x", 2), ("on_x", 0, 4), ("on_x", 0, 5),
+        ("form", 0, 0), ("on_x", 1, 4), ("on_x", 1, 5), ("send_b", 2), ("form", 0, 1),
+        ("own_x", 3), ("up_y", 0), ("down_y", 0), ("on_x", 2, 4), ("on_x", 2, 5),
+        ("up_z", 0), ("form", 1, 0), ("share_up", 0), ("down_z", 0), ("share_down", 0),
+        ("own_y", 1), ("on_x", 3, 4), ("on_x", 3, 5), ("form", 1, 1), ("send_b", 3),
+        ("on_x", 0, 8), ("on_x", 0, 9), ("form", 2, 0), ("up_z", 1), ("on_x", 0, 12),
+        ("on_x", 0, 13), ("form", 2, 1), ("share_far", 0), ("share_up", 1), ("far_y", 0),
+        ("send_b", 4), ("down_z", 1), ("share_down", 1), ("up_z", 2), ("up_y", 1),
+        ("down_y", 1), ("form", 3, 0), ("on_x", 0, 16), ("on_x", 0, 17), ("own_y", 2),
+        ("down_z", 2), ("share_down", 2), ("share_up", 2), ("form", 3, 1), ("on_x", 1, 8),
+        ("on_x", 1, 9), ("send_b", 5), ("share_far", 1), ("form", 4, 0), ("on_x", 1, 12),
+        ("on_x", 1, 13), ("up_z", 3),
     ],
     1: [
-        ("share_far", 2),
+        ("form", 4, 1), ("far_y", 1), ("share_far", 2), ("share_up", 3), ("up_y", 2),
+        ("down_y", 2), ("down_z", 3), ("share_down", 3), ("up_z", 4), ("send_b", 6),
     ],
     2: [
-        ("form", 5, 0), ("on_x", 2, 8), ("on_x", 2, 9), ("send_b", 6),
+        ("form", 5, 0), ("own_y", 3), ("on_x", 1, 16), ("on_x", 1, 17), ("form", 5, 1),
+        ("down_z", 4), ("share_down", 4), ("share_up", 4), ("far_y", 2), ("send_b", 7),
+        ("on_x", 2, 8), ("on_x", 2, 9), ("share_far", 3), ("form", 6, 0), ("on_x", 2, 12),
+        ("on_x", 2, 13), ("up_z", 5),
     ],
     3: [
-        ("up_z", 4),
+        ("form", 6, 1), ("down_z", 5), ("share_down", 5), ("share_up", 5), ("on_x", 2, 16),
+        ("on_x", 2, 17), ("up_y", 3), ("down_y", 3),
     ],
     4: [
-        ("form", 5, 1), ("far_y", 2), ("on_x", 2, 12), ("on_x", 2, 13),
+        ("share_far", 4), ("up_z", 6), ("form", 7, 0), ("form", 7, 1), ("far_y", 3),
+        ("down_z", 6), ("share_down", 6), ("share_up", 6), ("on_x", 3, 8), ("on_x", 3, 9),
     ],
     5: [
-        ("share_up", 4), ("share_far", 3), ("send_b", 7),
+        ("share_far", 5), ("on_x", 3, 12), ("on_x", 3, 13), ("up_z", 7), ("on_x", 3, 16),
+        ("on_x", 3, 17),
     ],
     6: [
-        ("up_y", 3), ("down_y", 3), ("up_z", 5), ("down_z", 4), ("share_down", 4),
-    ],
-    8: [
-        ("on_x", 2, 16), ("on_x", 2, 17),
-    ],
-    9: [
-        ("form", 6, 0),
-    ],
-    11: [
-        ("form", 6, 1), ("share_up", 5), ("down_z", 5), ("share_down", 5), ("on_x", 3, 8),
-        ("on_x", 3, 9),
-    ],
-    13: [
-        ("form", 7, 0), ("share_far", 4), ("on_x", 3, 12), ("on_x", 3, 13),
-    ],
-    14: [
-        ("form", 7, 1), ("up_z", 6),
-    ],
-    15: [
-        ("far_y", 3),
-    ],
-    17: [
-        ("share_up", 6), ("down_z", 6), ("share_down", 6),
-    ],
-    19: [
-        ("up_z", 7), ("share_far", 5),
-    ],
-    20: [
-        ("on_x", 3, 16), ("on_x", 3, 17), ("share_up", 7),
-    ],
-    22: [
-        ("down_z", 7), ("share_down", 7),
-    ],
-    24: [
-        ("share_far", 6),
-    ],
-    25: [
+        ("down_z", 7), ("share_down", 7), ("share_up", 7), ("share_far", 6),
+    ],
+    7: [
         ("share_far", 7),
     ],
 }

time: 113 us -> 102 us (0.903)
  Pallas kernels: 113 us -> 102 us
    pallas_call x1, Pallas kernels: 106 us -> 95.3 us  [per_device(): pl.pallas_call(kernel, out_shape=jax.ShapeDtypeStruct((IRREPS, OCC, WIDTH...]
where the time goes in v3:
time: 102 us
  Pallas kernels  102 us (100%)
    pallas_call x1, Pallas kernels, per_device(): pl.pallas_call(kernel, out_shape=jax.ShapeDtypeStruct((IRREPS, OCC, WIDTH...  95.3 us
    pallas_call x1, Pallas kernels, per_device(): pl.pallas_call(interleave, out_shape=jax.ShapeDtypeStruct((OCC * IRREPS,...  6.62 us

profile of v3, /device:TPU:1, one launch (start us, length us, event | category | flops | bytes accessed | tf_op | source)
XLA Modules:
  0.0 102.0 jit_solution(1952775590795910386)
XLA Ops:
  0.0 95.3 %shard_map.46.in_ref = bf16[8,512,1024]{2,1,0:T(8,128)(2,1)} custom-call(s32[8]{0:T(128)} %cd_hbm.1, s32[8]{0:T(128)} %ab_hbm.1, bf16[4,128,512]{2,1,0:T(8,128)(2,1)} %bitcast.4, bf16[8,128,1024]{2,1,0:T(8,128)(2,1)} %ints_ref.1), custom_call_target="tpu_custom_call" | custom-call | flops 18253611008 | bytes 12582912 | tf_op jit(solution)/shard_map/pallas_call | solution.py:377
  95.3 6.6 %shard_map.47 = bf16[4096,1024]{1,0:T(8,128)(2,1)} custom-call(bf16[8,512,1024]{2,1,0:T(8,128)(2,1)} %shard_map.46.in_ref), custom_call_target="tpu_custom_call" | custom-call | tf_op jit(solution)/shard_map/pallas_call | solution.py:414

commit v4 on v3

--- a/solution.py
+++ b/solution.py
@@ -75,8 +75,8 @@
 
 def kernel(
     cd_hbm, ab_hbm, amps_ref, ints_ref, out_ref,
-    cd_ref, ab_ref, a_mine, a_all, b_mine, b_other, d_all, peaks, peaks_other, rows_up, scales, a_now, partial, staged,
-    b_send, b_recv, d_send, d_recv, a_send, a_recv, s_send, s_recv, here_sem, out_sem,
+    cd_ref, ab_ref, a_mine, a_all, b_mine, b_other, d_all, peaks, peaks_other, rows_up, scales, a_now, partial,
+    b_send, b_recv, d_send, d_recv, a_send, a_recv, s_send, s_recv, here_sem,
 ):
     row, col = lax.axis_index("row"), lax.axis_index("col")
     y, x = row // SIDE, lax.rem(row, SIDE)
@@ -245,19 +245,11 @@
     def strip(n):
         return pl.ds(pl.multiple_of(n * TILE, TILE), TILE)
 
-    def out_copy(g, n):
-        parity = lax.rem(g, 2)
-        return pltpu.make_async_copy(
-            staged.at[parity, n], out_ref.at[g, :, strip(n)], out_sem.at[parity, n]
-        )
-
     def multiply_most(g, n):
         partial[n] = product(g, (0, 1, 2), strip(n))
 
     def multiply_rest(g, n):
-        pl.when(g >= 2)(lambda: out_copy(g - 2, n).wait())
-        staged[lax.rem(g, 2), n] = (partial[n] + product(g, (3,), strip(n))).astype(jnp.bfloat16)
-        out_copy(g, n).start()
+        out_ref[g, :, strip(n)] = (partial[n] + product(g, (3,), strip(n))).astype(jnp.bfloat16)
 
     for load in loads[1:]:
         load.wait()
@@ -344,29 +336,20 @@
 
     lax.fori_loop(0, IRREPS, drain_b, 0)
     lax.fori_loop(0, PAIRS, drain_a, 0)
-    for n in range(STRIPS):
-        out_copy(IRREPS - 2, n).wait()
-        out_copy(IRREPS - 1, n).wait()
-
-
-def interleave(in_ref, out_ref, taken, given, in_sem, out_sem):
-    def take(n):
-        return pltpu.make_async_copy(in_ref.at[:, pl.ds(n * SLAB, SLAB), :], taken.at[n], in_sem.at[n])
-
+
+
+def interleave(in_ref, out_ref, given, out_sem):
     def give(n):
         rows = pl.ds(pl.multiple_of(n * (SLAB * IRREPS), SLAB * IRREPS), SLAB * IRREPS)
         return pltpu.make_async_copy(given.at[n], out_ref.at[rows], out_sem.at[n])
 
-    slabs = OCC // SLAB
-    for n in range(slabs):
-        take(n).start()
-
     def slab(n, _):
-        take(n).wait()
-        given[n] = jnp.swapaxes(taken[n], 0, 1).reshape(SLAB * IRREPS, WIDTH)
+        rows = pl.ds(pl.multiple_of(n * SLAB, SLAB), SLAB)
+        given[n] = jnp.swapaxes(in_ref[:, rows, :], 0, 1).reshape(SLAB * IRREPS, WIDTH)
         give(n).start()
         return 0
 
+    slabs = OCC // SLAB
     lax.fori_loop(0, slabs, slab, 0)
     for n in range(slabs):
         give(n).wait()
@@ -376,9 +359,9 @@
     pairs = amplitudes.transpose(1, 2, 0).reshape(PAIRS, DEPTH, OCC)
     by_irrep = pl.pallas_call(
         kernel,
-        out_shape=jax.ShapeDtypeStruct((IRREPS, OCC, WIDTH), jnp.bfloat16),
-        in_specs=[pl.BlockSpec(memory_space=pl.ANY)] * 4,
-        out_specs=pl.BlockSpec(memory_space=pl.ANY),
+        out_shape=pltpu.VMEM((IRREPS, OCC, WIDTH), jnp.bfloat16),
+        in_specs=[pl.BlockSpec(memory_space=pltpu.HBM)] * 4,
+        out_specs=pl.BlockSpec(memory_space=pltpu.VMEM),
         scratch_shapes=[
             pltpu.SMEM((IRREPS,), jnp.int32),
             pltpu.SMEM((IRREPS,), jnp.int32),
@@ -393,7 +376,6 @@
             pltpu.VMEM((8, IRREPS, DEPTH), jnp.float32),
             pltpu.VMEM((OCC, 8 * DEPTH), jnp.bfloat16),
             pltpu.VMEM((STRIPS, OCC, TILE), jnp.float32),
-            pltpu.VMEM((2, STRIPS, OCC, TILE), jnp.bfloat16),
             pltpu.SemaphoreType.DMA((IRREPS, 2)),
             pltpu.SemaphoreType.DMA((IRREPS, 2)),
             pltpu.SemaphoreType.DMA((IRREPS, D_KINDS)),
@@ -403,27 +385,24 @@
             pltpu.SemaphoreType.DMA((8,)),
             pltpu.SemaphoreType.DMA((8,)),
             pltpu.SemaphoreType.DMA((4,)),
-            pltpu.SemaphoreType.DMA((2, STRIPS)),
         ],
         compiler_params=pltpu.CompilerParams(
-            collective_id=0, has_side_effects=True, vmem_limit_bytes=60 << 20
+            collective_id=0, has_side_effects=True, vmem_limit_bytes=48 << 20
         ),
         cost_estimate=pl.CostEstimate(flops=17 << 30, bytes_accessed=12 << 20, transcendentals=0),
-    )(cd_count, ab_count, pairs, integrals)
+    )(*(pltpu.with_memory_space_constraint(v, pltpu.HBM) for v in (cd_count, ab_count, pairs, integrals)))
     slabs = OCC // SLAB
     ladder = pl.pallas_call(
         interleave,
         out_shape=jax.ShapeDtypeStruct((OCC * IRREPS, WIDTH), jnp.bfloat16),
-        in_specs=[pl.BlockSpec(memory_space=pl.ANY)],
+        in_specs=[pl.BlockSpec(memory_space=pltpu.VMEM)],
         out_specs=pl.BlockSpec(memory_space=pl.ANY),
         scratch_shapes=[
-            pltpu.VMEM((slabs, IRREPS, SLAB, WIDTH), jnp.bfloat16),
             pltpu.VMEM((slabs, SLAB * IRREPS, WIDTH), jnp.bfloat16),
             pltpu.SemaphoreType.DMA((slabs,)),
-            pltpu.SemaphoreType.DMA((slabs,)),
         ],
-        compiler_params=pltpu.CompilerParams(vmem_limit_bytes=60 << 20),
-    )(by_irrep)
+        compiler_params=pltpu.CompilerParams(vmem_limit_bytes=16 << 20),
+    )(pltpu.with_memory_space_constraint(by_irrep, pltpu.VMEM))
     return ladder.reshape(OCC, IRREPS, WIDTH)
 
 

time: 102 us -> 98.3 us (0.964)
  Pallas kernels: 102 us -> 98.2 us
    pallas_call x1, Pallas kernels: 6.62 us -> 3.54 us  [per_device(): pl.pallas_call(interleave, out_shape=jax.ShapeDtypeStruct((OCC * IRREPS,...]
where the time goes in v4:
time: 98.3 us; the launch traced here: 98.2 us
  Pallas kernels  98.2 us (100%)
    pallas_call x1, Pallas kernels, per_device(): pl.pallas_call(kernel, out_shape=pltpu.VMEM((IRREPS, OCC, WIDTH), jnp.bfl...  94.6 us
    pallas_call x1, Pallas kernels, per_device(): pl.pallas_call(interleave, out_shape=jax.ShapeDtypeStruct((OCC * IRREPS,...  3.54 us

profile of v4, /device:TPU:1, one launch (start us, length us, event | category | flops | bytes accessed | tf_op | source)
XLA Modules:
  0.0 98.2 jit_solution(8091883299901960990)
XLA Ops:
  0.0 94.6 %shard_map.46.in_ref = bf16[8,512,1024]{2,1,0:T(8,128)(2,1)S(1)} custom-call(s32[8]{0:T(128)} %cd_hbm.1, s32[8]{0:T(128)} %ab_hbm.1, bf16[4,128,512]{2,1,0:T(8,128)(2,1)} %bitcast.4, bf16[8,128,1024]{2,1,0:T(8,128)(2,1)} %ints_ref.1), custom_call_target="tpu_custom_call" | custom-call | flops 18253611008 | bytes 12582912 | tf_op jit(solution)/shard_map/pallas_call | solution.py:360
  94.6 3.5 %shard_map.47 = bf16[4096,1024]{1,0:T(8,128)(2,1)} custom-call(bf16[8,512,1024]{2,1,0:T(8,128)(2,1)S(1)} %shard_map.46.in_ref), custom_call_target="tpu_custom_call" | custom-call | tf_op jit(solution)/shard_map/pallas_call | solution.py:395

commit v5 on v4

--- a/solution.py
+++ b/solution.py
@@ -189,7 +189,11 @@
         whole_number = jnp.round(jnp.minimum(scaled, 32767.0)).astype(jnp.int32)
         d_all[g, col, halves[h], :] = whole_number.astype(jnp.int16)
         d_copy(g, h).start()
-        d_copy(g, 2 + h).start()
+        if g == 0:
+            d_copy(g, 2 + h).start()
+        elif h == 1:
+            d_copy(g, 3).start()
+            d_copy(g, 2).start()
         if h == 1:
             d_copy(g, 6).start()
 
@@ -287,6 +291,16 @@
     for n in range(7):
         s_copy(n, col).start()
 
+    def sent_blocks(g, kinds=D_KINDS):
+        b_copy(g, 0).wait_send()
+        b_copy(g, 1).wait_send()
+        for kind in range(kinds):
+            d_copy(g, kind).wait_send()
+
+    def sent_pair(p):
+        for kind in range(A_KINDS):
+            a_copy(p, kind).wait_send()
+
     def unit(i, _):
         for at, calls in PLAN.items():
             @pl.when(i == at)
@@ -299,6 +313,17 @@
             sender = [slot(-1, core), slot(-2, core), slot(-3, core)] + [slot(-n, other) for n in (0, 1, 2, 3)]
             for n in range(7):
                 s_copy(n, sender[n]).wait_recv()
+                s_copy(n, col).wait_send()
+            peak_copy.wait_send()
+
+        pl.when((i >= 2) & (i < IRREPS))(lambda: sent_blocks(i - 2))
+        pl.when((i >= 3) & (i < IRREPS) & (lax.rem(i, 2) == 1))(lambda: sent_pair((i - 3) // 2))
+
+        @pl.when(i == IRREPS)
+        def _():
+            sent_blocks(IRREPS - 2)
+            sent_pair(PAIRS - 1)
+            sent_blocks(IRREPS - 1, D_KINDS - 1)
 
         g, n = i // STRIPS, lax.rem(i, STRIPS)
         last = IRREPS * STRIPS
@@ -318,24 +343,7 @@
 
     lax.fori_loop(0, UNITS, unit, 0)
 
-    for n in range(7):
-        s_copy(n, col).wait_send()
-    peak_copy.wait_send()
-
-    def drain_b(g, _):
-        b_copy(g, 0).wait_send()
-        b_copy(g, 1).wait_send()
-        for kind in range(D_KINDS):
-            d_copy(g, kind).wait_send()
-        return 0
-
-    def drain_a(p, _):
-        for kind in range(A_KINDS):
-            a_copy(p, kind).wait_send()
-        return 0
-
-    lax.fori_loop(0, IRREPS, drain_b, 0)
-    lax.fori_loop(0, PAIRS, drain_a, 0)
+    d_copy(IRREPS - 1, D_KINDS - 1).wait_send()
 
 
 def interleave(in_ref, out_ref, given, out_sem):

time: 98.3 us -> 98.2 us (level)
  no operation moved by 1% of the time
where the time goes in v5:
time: 98.2 us; the launch traced here: 98.1 us
  Pallas kernels  98.1 us (100%)
    pallas_call x1, Pallas kernels, per_device(): pl.pallas_call(kernel, out_shape=pltpu.VMEM((IRREPS, OCC, WIDTH), jnp.bfl...  94.5 us
    pallas_call x1, Pallas kernels, per_device(): pl.pallas_call(interleave, out_shape=jax.ShapeDtypeStruct((OCC * IRREPS,...  3.54 us

profile of v5, /device:TPU:1, one launch (start us, length us, event | category | flops | bytes accessed | tf_op | source)
XLA Modules:
  0.0 98.1 jit_solution(11518730003235778087)
XLA Ops:
  0.0 94.5 %shard_map.46.in_ref = bf16[8,512,1024]{2,1,0:T(8,128)(2,1)S(1)} custom-call(s32[8]{0:T(128)} %cd_hbm.1, s32[8]{0:T(128)} %ab_hbm.1, bf16[4,128,512]{2,1,0:T(8,128)(2,1)} %bitcast.4, bf16[8,128,1024]{2,1,0:T(8,128)(2,1)} %ints_ref.1), custom_call_target="tpu_custom_call" | custom-call | flops 18253611008 | bytes 12582912 | tf_op jit(solution)/shard_map/pallas_call | solution.py:368
  94.6 3.5 %shard_map.47 = bf16[4096,1024]{1,0:T(8,128)(2,1)} custom-call(bf16[8,512,1024]{2,1,0:T(8,128)(2,1)S(1)} %shard_map.46.in_ref), custom_call_target="tpu_custom_call" | custom-call | tf_op jit(solution)/shard_map/pallas_call | solution.py:403
